TPU v7x, 512 devices: a whole 4x4x16 slice. The times are simulated.
512 devices in a mesh: ray: 32 (over z, y_lo), cell: 16 (over x, y_hi, core).
Axes of the slice: x: 4, y: 4 (y_hi: 2, y_lo: 2; y = y_hi * 2 + y_lo), z: 16, core: 2. Of those that a mesh axis runs over, the one named last changes fastest.
Arguments:
- tile_values: bfloat16 [256, 16, 4, 128, 128], P('ray', 'cell'), may hold values from -0.375 to 0.375
- tile_cols: int32 [256, 16, 4], P('ray', 'cell'), may hold values from 0 to 3, as said below
- tile_count: int32 [256, 16], P('ray', 'cell'), may hold values from 0 to 4
- ray_weight: float32 [32768], P('ray'), may hold values from 0.2 to 5
Outputs:
- hessian_blocks: float32 [4, 16, 512, 512], P(None, 'cell', 'ray')
Inputs may be any that keep to these rules, and one draw needn't show every extreme that they name: `tile_cols`: within one ray tile and panel the 4 slots name different cell tiles; slots at or beyond tile_count are padding and their tiles are not part of the Jacobian.
All inputs are finite; a program needn't handle non-finite values.
Results may differ from a plain program's by a relative error of at most 0.00094.
Values may be sent and summed in bfloat16 or wider, within the bound.
A program may use at most 64 MiB of HBM per device.

v0:
```python
import jax
import jax.numpy as jnp
from jax import lax
from jax.sharding import Mesh
from jax.sharding import PartitionSpec as P

TILE = 128
STEPS = 4
CT = 4
RAY = ("ray_0", "ray_1")


def passed_along(value, axis, steps):
    count = lax.axis_size(axis)
    pairs = [(source, (source + steps) % count) for source in range(count)]
    return lax.ppermute(value, axis, pairs)


def sum_by_axis(value, axes, dim):
    if not axes:
        return value
    nearer = lax.psum_scatter(value, axes[0], scatter_dimension=dim, tiled=True)
    return sum_by_axis(nearer, axes[1:], dim)


def place_table(columns, counts, panel_tiles):
    slot_index = jnp.arange(columns.shape[-1], dtype=jnp.int32)
    is_live = slot_index[None, :] < counts[:, None]
    is_match = columns[:, :, None] == jnp.arange(panel_tiles, dtype=jnp.int32)[None, None, :]
    return (is_match & is_live[:, :, None]).astype(jnp.bfloat16)


def placed_rows(values, table):
    spread = jnp.einsum("tki,tkra->tria", table, values, preferred_element_type=jnp.float32)
    return spread.astype(jnp.bfloat16).reshape(-1, CT * TILE)


def pair_block(own_placed, visit_values, visit_cols, visit_count):
    visit_placed = placed_rows(visit_values, place_table(visit_cols, visit_count, CT))
    return lax.dot_general(
        own_placed, visit_placed, (((0,), (0,)), ((), ())), preferred_element_type=jnp.float32
    )


def body(tile_values, tile_cols, tile_count, ray_weight):
    own_values = tile_values[:, 0]
    own_cols = tile_cols[:, 0]
    own_count = tile_count[:, 0]
    row_tiles = own_values.shape[0]
    weighted = (ray_weight.reshape(row_tiles, 1, TILE, 1) * own_values.astype(jnp.float32)).astype(
        jnp.bfloat16
    )
    own_placed = placed_rows(weighted, place_table(own_cols, own_count, CT))
    visiting = (own_values, own_cols, own_count)
    partials = []
    for cycle_step in range(STEPS):
        if cycle_step > 0:
            visiting = passed_along((visiting[0], visiting[1], visiting[2]), "cell", 1)
        partial_value = pair_block(own_placed, visiting[0], visiting[1], visiting[2])
        partials.append(partial_value)
    stacked = sum_by_axis(jnp.stack(partials), RAY, 1)
    return stacked[:, None]


def solution(mesh):
    finer = Mesh(mesh.devices.reshape(16, 2, mesh.shape["cell"]), ("ray_0", "ray_1", "cell"))
    return jax.shard_map(
        body,
        mesh=finer,
        in_specs=(P(RAY, "cell", None, None, None), P(RAY, "cell", None), P(RAY, "cell"), P(RAY)),
        out_specs=P(None, "cell", RAY, None),
        check_vma=False,
    )
```

profile of v0, /device:TPU:1, one launch (start us, length us, event | category | flops | bytes accessed | tf_op | source)
XLA Modules:
  0.0 201.3 jit_solution(803648773922548176)
XLA Ops:
  6.5 0.0 copy-start
  6.5 0.0 reduce-scatter.3.cloned.1.call-start
  6.5 2.1 %copy.57 = bf16[8,1,4,128,128]{4,2,3,0,1:T(4,128)(2,1)S(1)} copy(bf16[8,1,4,128,128]{4,3,2,1,0:T(8,128)(2,1)} %param.4) | data formatting | bytes 2097152 | tf_op args[0]
  8.7 6.2 %collective-permute-start.2 = (bf16[8,4,128,128]{3,1,2,0:T(4,128)(2,1)S(1)}, bf16[8,4,128,128]{3,1,2,0:T(4,128)(2,1)S(1)}, u32[]{:S(2)}, u32[]{:S(2)}) collective-permute-start(bf16[8,4,128,128]{3,1,2,0:T(4,128)(2,1)S(1)} %bitcast.81), channel_id=1, source_target_pairs={{0,1},{1,2},{2,3},{3,4},{4,5},{5,6},{6,7},{7,8},{8,9},{9,10},{10,1... | collective-permute-start | bytes 3145736 | tf_op jit(solution)/shard_map/ppermute | solution.py:16
  14.9 1.9 collective-permute-start.1
  16.8 3.3 %collective-permute-start = (s32[8,4]{0,1:T(4,128)}, s32[8,4]{0,1:T(4,128)S(1)}, u32[]{:S(2)}, u32[]{:S(2)}) collective-permute-start(s32[8,4]{0,1:T(4,128)} %bitcast.85), channel_id=1, source_target_pairs={{0,1},{1,2},{2,3},{3,4},{4,5},{5,6},{6,7},{7,8},{8,9},{9,10},{10,1... | collective-permute-start | bytes 392 | tf_op jit(solution)/shard_map/ppermute | solution.py:16
  20.1 0.8 copy.6
  20.9 0.7 iota_compare_fusion.7
  21.6 2.6 %convolution_convert_fusion.4 = bf16[8,128,128,4]{2,3,1,0:T(4,128)(2,1)S(1)} fusion(f32[8,128]{1,0:T(8,128)} %bitcast.87, s32[8,4]{1,0:T(8,128)S(1)} %copy.6, pred[8,4]{1,0:T(8,128)(4,1)S(1)} %iota_compare_fusion.7, bf16[8,1,4,128,128]{4,3,2,1,0:T(8,128)(2,1)} %param.4), kind=kOutput, calls=%fused_computation.6 | convolution fusion | flops 6291712 | bytes 2101408 | tf_op jit(solution)/shard_map/tki,tkra->tria/dot_general | solution.py:34
  24.2 0.0 copy-start.1
  24.2 2.4 %collective-permute-done.2 = bf16[8,4,128,128]{3,1,2,0:T(4,128)(2,1)S(1)} collective-permute-done((bf16[8,4,128,128]{3,1,2,0:T(4,128)(2,1)S(1)}, bf16[8,4,128,128]{3,1,2,0:T(4,128)(2,1)S(1)}, u32[]{:S(2)}, u32[]{:S(2)}) %collective-permute-start.2) | collective-permute-done | bytes 1048608 | tf_op jit(solution)/shard_map/ppermute | solution.py:16
  26.6 5.9 %collective-permute-start.5 = (bf16[8,4,128,128]{3,1,2,0:T(4,128)(2,1)S(1)}, bf16[8,4,128,128]{3,1,2,0:T(4,128)(2,1)S(1)}, u32[]{:S(2)}, u32[]{:S(2)}) collective-permute-start(bf16[8,4,128,128]{3,1,2,0:T(4,128)(2,1)S(1)} %collective-permute-done.2), channel_id=1, source_target_pairs={{0,1},{1,2},{2,3},{3,4},{4,5},{5,6},{6,7},{7,8},{8,9},{9,10},{10,1... | collective-permute-start | bytes 3145736 | tf_op jit(solution)/shard_map/ppermute | solution.py:16
  32.5 0.0 copy-done
  32.5 0.9 convolution_convert_fusion.3
  33.4 0.7 convolution_bitcast_fusion.3
  34.2 0.0 collective-permute-done.1
  34.2 1.9 collective-permute-start.4
  36.1 0.1 iota_compare_fusion.6
  36.2 8.1 %collective-permute-done.4 = s32[8]{0:T(128)S(1)} collective-permute-done((s32[8]{0:T(128)S(1)}, s32[8]{0:T(128)S(1)}, u32[]{:S(2)}, u32[]{:S(2)}) %collective-permute-start.4) | collective-permute-done | bytes 64 | tf_op jit(solution)/shard_map/ppermute | solution.py:16
  44.3 0.1 iota_compare_fusion.5
  44.3 5.9 %collective-permute-start.7 = (s32[8]{0:T(128)S(1)}, s32[8]{0:T(128)S(1)}, u32[]{:S(2)}, u32[]{:S(2)}) collective-permute-start(s32[8]{0:T(128)S(1)} %collective-permute-done.4), channel_id=1, source_target_pairs={{0,1},{1,2},{2,3},{3,4},{4,5},{5,6},{6,7},{7,8},{8,9},{9,10},{10,1... | collective-permute-start | bytes 104 | tf_op jit(solution)/shard_map/ppermute | solution.py:16
  50.2 0.0 collective-permute-done
  50.3 1.9 collective-permute-start.3
  52.2 5.5 %collective-permute-done.7 = s32[8]{0:T(128)S(1)} collective-permute-done((s32[8]{0:T(128)S(1)}, s32[8]{0:T(128)S(1)}, u32[]{:S(2)}, u32[]{:S(2)}) %collective-permute-start.7) | collective-permute-done | bytes 64 | tf_op jit(solution)/shard_map/ppermute | solution.py:16
  57.6 0.1 iota_compare_fusion.4
  57.7 1.9 collective-permute-done.3
  59.6 0.0 copy-done.1
  59.6 1.9 collective-permute-start.6
  61.5 0.1 copy.7
  61.6 0.1 copy.8
  61.7 6.4 %collective-permute-done.6 = s32[8,4]{0,1:T(4,128)S(1)} collective-permute-done((s32[8,4]{0,1:T(4,128)S(1)}, s32[8,4]{0,1:T(4,128)S(1)}, u32[]{:S(2)}, u32[]{:S(2)}) %collective-permute-start.6) | collective-permute-done | bytes 160 | tf_op jit(solution)/shard_map/ppermute | solution.py:16
  68.1 0.1 copy.9
  68.2 0.0 copy-start.2
  68.2 0.0 collective-permute-done.5
  68.2 2.0 %collective-permute-start.8 = (bf16[8,4,128,128]{3,1,2,0:T(4,128)(2,1)S(1)}, bf16[8,4,128,128]{3,1,2,0:T(4,128)(2,1)S(1)}, u32[]{:S(2)}, u32[]{:S(2)}) collective-permute-start(bf16[8,4,128,128]{3,1,2,0:T(4,128)(2,1)S(1)} %collective-permute-done.5), channel_id=1, source_target_pairs={{0,1},{1,2},{2,3},{3,4},{4,5},{5,6},{6,7},{7,8},{8,9},{9,10},{10,1... | collective-permute-start | bytes 3145736 | tf_op jit(solution)/shard_map/ppermute | solution.py:16
  70.3 0.7 convolution_convert_fusion.2
  71.0 2.0 convolution_bitcast_fusion.2
  72.9 0.7 convolution_convert_fusion.1
  73.6 0.0 copy-done.2
  73.6 0.7 convolution_bitcast_fusion.1
  74.4 7.6 %collective-permute-done.8 = bf16[8,4,128,128]{3,1,2,0:T(4,128)(2,1)S(1)} collective-permute-done((bf16[8,4,128,128]{3,1,2,0:T(4,128)(2,1)S(1)}, bf16[8,4,128,128]{3,1,2,0:T(4,128)(2,1)S(1)}, u32[]{:S(2)}, u32[]{:S(2)}) %collective-permute-start.8) | collective-permute-done | bytes 1048608 | tf_op jit(solution)/shard_map/ppermute | solution.py:16
  82.0 0.7 convolution_convert_fusion
  82.7 0.7 convolution_bitcast_fusion
  83.4 2.4 %pad_maximum_fusion = f32[4,512,512]{2,1,0:T(8,128)} fusion(f32[1,512,512]{2,1,0:T(8,128)S(1)} %convolution_bitcast_fusion, f32[1,512,512]{2,1,0:T(8,128)S(1)} %convolution_bitcast_fusion.1, f32[1,512,512]{2,1,0:T(8,128)S(1)} %convolution_bitcast_fusion.2, f32[1,512,512]{2,1,0:T(8,128)S(1)} %convolution_bitcast_fusion.3), kind=kLoop, calls=%fused_computation | loop fusion | flops 3145728 | bytes 8388608 | tf_op jit(solution)/shard_map/stack | solution.py:61
  85.8 0.0 reduce-scatter.3.cloned.1.call-update
  85.8 0.0 reduce-scatter.5.cloned.1.call-start
  85.9 76.6 %reduce-scatter.3.cloned.1.call-done = f32[4,32,512]{2,1,0:T(8,128)} async-done(((f32[4,512,512]{2,1,0:T(8,128)}), f32[4,32,512]{2,1,0:T(8,128)}) %reduce-scatter.3.cloned.1.call-update) | async-done | bytes 262160 | tf_op jit(solution)/shard_map/reduce_scatter | solution.py:22
  162.5 0.0 reduce-scatter.5.cloned.1.call-update
  162.5 32.0 %reduce-scatter.5.cloned.1.call-done = f32[4,16,512]{2,1,0:T(8,128)} async-done(((f32[4,32,512]{2,1,0:T(8,128)}), f32[4,16,512]{2,1,0:T(8,128)}) %reduce-scatter.5.cloned.1.call-update) | async-done | bytes 131088 | tf_op jit(solution)/shard_map/reduce_scatter | solution.py:22
Async XLA Ops:
  6.5 26.0 %copy-start = (bf16[8,1,4,128,128]{4,3,2,1,0:T(8,128)(2,1)S(1)}, bf16[8,1,4,128,128]{4,3,2,1,0:T(8,128)(2,1)}, u32[]{:S(2)}) copy-start(bf16[8,1,4,128,128]{4,3,2,1,0:T(8,128)(2,1)} %param.4) | copy-start | bytes 3145732
  6.5 156.0 %reduce-scatter.3.cloned.1.call-start = ((), (), s32[]{:S(2)}) async-start(), calls=%async_computation.2 | async-start | bytes 4456448 | tf_op jit(solution)/shard_map/reduce_scatter | solution.py:22
  8.7 17.9 %collective-permute-start.2 = (bf16[8,4,128,128]{3,1,2,0:T(4,128)(2,1)S(1)}, bf16[8,4,128,128]{3,1,2,0:T(4,128)(2,1)S(1)}, u32[]{:S(2)}, u32[]{:S(2)}) collective-permute-start(bf16[8,4,128,128]{3,1,2,0:T(4,128)(2,1)S(1)} %bitcast.81), channel_id=1, source_target_pairs={{0,1},{1,2},{2,3},{3,4},{4,5},{5,6},{6,7},{7,8},{8,9},{9,10},{10,1... | collective-permute-start | bytes 3145736 | tf_op jit(solution)/shard_map/ppermute | solution.py:16
  14.9 19.3 %collective-permute-start.1 = (s32[8]{0:T(128)}, s32[8]{0:T(128)S(1)}, u32[]{:S(2)}, u32[]{:S(2)}) collective-permute-start(s32[8]{0:T(128)} %bitcast.88), channel_id=1, source_target_pairs={{0,1},{1,2},{2,3},{3,4},{4,5},{5,6},{6,7},{7,8},{8,9},{9,10},{10,1... | collective-permute-start | bytes 104 | tf_op jit(solution)/shard_map/ppermute | solution.py:16
  16.8 33.4 %collective-permute-start = (s32[8,4]{0,1:T(4,128)}, s32[8,4]{0,1:T(4,128)S(1)}, u32[]{:S(2)}, u32[]{:S(2)}) collective-permute-start(s32[8,4]{0,1:T(4,128)} %bitcast.85), channel_id=1, source_target_pairs={{0,1},{1,2},{2,3},{3,4},{4,5},{5,6},{6,7},{7,8},{8,9},{9,10},{10,1... | collective-permute-start | bytes 392 | tf_op jit(solution)/shard_map/ppermute | solution.py:16
  24.2 35.4 %copy-start.1 = (bf16[8,128,128,4]{2,3,1,0:T(4,128)(2,1)}, bf16[8,128,128,4]{2,3,1,0:T(4,128)(2,1)S(1)}, u32[]{:S(2)}) copy-start(bf16[8,128,128,4]{2,3,1,0:T(4,128)(2,1)S(1)} %convolution_convert_fusion.4) | copy-start | bytes 3145732
  26.6 41.6 %collective-permute-start.5 = (bf16[8,4,128,128]{3,1,2,0:T(4,128)(2,1)S(1)}, bf16[8,4,128,128]{3,1,2,0:T(4,128)(2,1)S(1)}, u32[]{:S(2)}, u32[]{:S(2)}) collective-permute-start(bf16[8,4,128,128]{3,1,2,0:T(4,128)(2,1)S(1)} %collective-permute-done.2), channel_id=1, source_target_pairs={{0,1},{1,2},{2,3},{3,4},{4,5},{5,6},{6,7},{7,8},{8,9},{9,10},{10,1... | collective-permute-start | bytes 3145736 | tf_op jit(solution)/shard_map/ppermute | solution.py:16
  34.2 10.1 %collective-permute-start.4 = (s32[8]{0:T(128)S(1)}, s32[8]{0:T(128)S(1)}, u32[]{:S(2)}, u32[]{:S(2)}) collective-permute-start(s32[8]{0:T(128)S(1)} %collective-permute-done.1), channel_id=1, source_target_pairs={{0,1},{1,2},{2,3},{3,4},{4,5},{5,6},{6,7},{7,8},{8,9},{9,10},{10,1... | collective-permute-start | bytes 104 | tf_op jit(solution)/shard_map/ppermute | solution.py:16
  44.3 13.3 %collective-permute-start.7 = (s32[8]{0:T(128)S(1)}, s32[8]{0:T(128)S(1)}, u32[]{:S(2)}, u32[]{:S(2)}) collective-permute-start(s32[8]{0:T(128)S(1)} %collective-permute-done.4), channel_id=1, source_target_pairs={{0,1},{1,2},{2,3},{3,4},{4,5},{5,6},{6,7},{7,8},{8,9},{9,10},{10,1... | collective-permute-start | bytes 104 | tf_op jit(solution)/shard_map/ppermute | solution.py:16
  50.3 9.4 %collective-permute-start.3 = (s32[8,4]{0,1:T(4,128)S(1)}, s32[8,4]{0,1:T(4,128)S(1)}, u32[]{:S(2)}, u32[]{:S(2)}) collective-permute-start(s32[8,4]{0,1:T(4,128)S(1)} %collective-permute-done), channel_id=1, source_target_pairs={{0,1},{1,2},{2,3},{3,4},{4,5},{5,6},{6,7},{7,8},{8,9},{9,10},{10,1... | collective-permute-start | bytes 392 | tf_op jit(solution)/shard_map/ppermute | solution.py:16
  59.6 8.5 %collective-permute-start.6 = (s32[8,4]{0,1:T(4,128)S(1)}, s32[8,4]{0,1:T(4,128)S(1)}, u32[]{:S(2)}, u32[]{:S(2)}) collective-permute-start(s32[8,4]{0,1:T(4,128)S(1)} %collective-permute-done.3), channel_id=1, source_target_pairs={{0,1},{1,2},{2,3},{3,4},{4,5},{5,6},{6,7},{7,8},{8,9},{9,10},{10,1... | collective-permute-start | bytes 392 | tf_op jit(solution)/shard_map/ppermute | solution.py:16
  68.2 5.4 %copy-start.2 = (bf16[8,128,128,4]{2,3,1,0:T(4,128)(2,1)S(1)}, bf16[8,128,128,4]{2,3,1,0:T(4,128)(2,1)}, u32[]{:S(2)}) copy-start(bf16[8,128,128,4]{2,3,1,0:T(4,128)(2,1)} %copy-done.1) | copy-start | bytes 3145732
  68.2 13.8 %collective-permute-start.8 = (bf16[8,4,128,128]{3,1,2,0:T(4,128)(2,1)S(1)}, bf16[8,4,128,128]{3,1,2,0:T(4,128)(2,1)S(1)}, u32[]{:S(2)}, u32[]{:S(2)}) collective-permute-start(bf16[8,4,128,128]{3,1,2,0:T(4,128)(2,1)S(1)} %collective-permute-done.5), channel_id=1, source_target_pairs={{0,1},{1,2},{2,3},{3,4},{4,5},{5,6},{6,7},{7,8},{8,9},{9,10},{10,1... | collective-permute-start | bytes 3145736 | tf_op jit(solution)/shard_map/ppermute | solution.py:16
  85.8 108.6 %reduce-scatter.5.cloned.1.call-start = ((), (), s32[]{:S(2)}) async-start(), calls=%async_computation.3 | async-start | bytes 393216 | tf_op jit(solution)/shard_map/reduce_scatter | solution.py:22
Sparse Core Ops, SparseCore 0:
  86.0 76.4 reduce-scatter.2
  165.3 29.1 reduce-scatter.4
where the time goes:
time: 202 us; the launch traced here: 201 us
  waiting for transfers between devices  140 us (69%)
  starting transfers between devices  31 us (15%)
  between operations  13.6 us (7%)
  matrix products  9.79 us (5%)
  other arithmetic  3.34 us (2%)
  local copies, waits for them, and re-layouts  3.15 us (2%)
    reduce_scatter x2, waiting for transfers between devices, sum_by_axis(): nearer = lax.psum_scatter(value, axes[0], scatter_dimension=dim, tiled=True)  109 us
    ppermute x9, waiting for transfers between devices, passed_along(): return lax.ppermute(value, axis, pairs)  31.8 us
    ppermute x9, starting transfers between devices, passed_along(): return lax.ppermute(value, axis, pairs)  31 us
    dot_general x5, matrix products, placed_rows(): jnp.einsum('tki,tkra->tria', table, values, preferred_element_type=jnp.fl...  5.61 us
    dot_general x4, matrix products, pair_block(): lax.dot_general(own_placed, visit_placed, (((0,), (0,)), ((), ())), prefe...  4.18 us
  transfers between devices with their start and end apart: 11, of which 8 were waited for; matrix products, arithmetic and copies ran while one was open for 5% of the time, Pallas kernels for 0%

commit v1 on v0

v1 whole, which is shorter than its diff:
```python
import functools

import jax
import jax.numpy as jnp
from jax import lax
from jax.experimental import pallas as pl
from jax.experimental.pallas import tpu as pltpu
from jax.sharding import PartitionSpec as P

MESH = pl.DeviceIdType.MESH
TILE = 128
K = 4
CT = 4
FULL = 32700.0
STEP = 64.0


def streams_of(size, stride, mirror):
    found = []
    half = size // 2
    for sign, reach in ((1, half), (-1, size - 1 - half)):
        for rest in range(stride):
            path = [o for o in range(reach, 0, -1) if o % stride == rest % stride]
            if path:
                found.append([o * sign * (-1 if mirror else 1) for o in path])
    return found


class Stage:
    def __init__(self, name, items, streams, refs):
        self.name, self.items, self.streams, self.refs = name, items, streams, refs
        self.first = []
        count = 0
        for path in streams:
            self.first.append(count)
            count += len(path)
        self.messages = count
        self.steps = max(len(path) for path in streams)


PLAN = (("a", 4, 2, False), ("b", 4, 2, True), ("c0", 2, 2, False), ("c1", 2, 2, True), ("c2", 2, 2, False), ("c3", 2, 2, True))


def coded(x):
    largest = jnp.max(jnp.max(jnp.abs(x), axis=0), axis=0, keepdims=True)
    power = jnp.floor(jnp.log2(jnp.maximum(largest, 1e-30)) * STEP) + 1.0
    codes = jnp.round(x * (jnp.exp2(power * (-1.0 / STEP)) * FULL)[None])
    return codes.astype(jnp.int32).astype(jnp.int16), power


def kernel(nz, plan, values, cols, count, weight, out, *scratch):
    n_stages = len(plan)
    (own_v, own_wt, got_z, got_sib, got_r, in_send, in_recv) = scratch[:7]
    per = scratch[7 : 7 + 8 * n_stages]
    (b_out, b_in, b_send, b_recv) = scratch[7 + 8 * n_stages :]
    stages = []
    for i, (name, items, stride, mirror) in enumerate(plan):
        stages.append(Stage(name, items, streams_of(nz, stride, mirror), per[8 * i : 8 * i + 8]))

    p = lax.axis_index("cell")
    ray = lax.axis_index("ray")
    n_cell = lax.axis_size("cell")
    z, yl = ray // 2, ray % 2
    odd = p % 2
    chunk = CT * TILE // nz

    def at_cell(shift):
        return {"ray": ray, "cell": lax.rem(p + shift + n_cell, n_cell)}

    def at_z(shift):
        return {"ray": lax.rem(z + shift + nz, nz) * 2 + yl, "cell": p}

    sibling = {"ray": ray, "cell": p + 1 - 2 * odd}
    across = {"ray": ray + 1 - 2 * yl, "cell": p}
    r_target = at_cell(2 * odd - 3)
    r_source = at_cell(2 * odd + 1)
    third = at_cell(6 * odd - 3)

    shifts = set()
    for stage in stages:
        for path in stage.streams:
            for i, o in enumerate(path):
                d = (path[i + 1] if i + 1 < len(path) else 0) - o
                shifts.update((d, -d))
    peers = [sibling, at_cell(2), at_cell(-2), third, across] + [at_z(d) for d in sorted(shifts)]
    barrier = pltpu.get_barrier_semaphore()
    for peer in peers:
        pl.semaphore_signal(barrier, inc=1, device_id=peer, device_id_type=MESH)

    row_tiles = values.shape[0]
    started = []

    def send(src, dst, ssem, rsem, to):
        copy = pltpu.make_async_remote_copy(
            src_ref=src, dst_ref=dst, send_sem=ssem, recv_sem=rsem, device_id=to, device_id_type=MESH
        )
        copy.start()
        started.append(copy)
        return copy

    def await_recv(dst, ssem, rsem):
        pltpu.make_async_remote_copy(
            src_ref=dst, dst_ref=dst, send_sem=ssem, recv_sem=rsem, device_id=sibling, device_id_type=MESH
        ).wait_recv()

    def placed(t, i):
        slot, live = jnp.int32(0), jnp.int32(0)
        for k in range(K):
            here = jnp.where((cols[t, k] == i) & (k < count[t]), 1, 0)
            slot += k * here
            live += here
        return values[t, slot].astype(jnp.float32) * live.astype(jnp.float32)

    def place(t, carry):
        for i in range(CT):
            own_v[i, pl.ds(pl.multiple_of(t * TILE, TILE), TILE), :] = placed(t, i).astype(jnp.bfloat16)
        return carry

    lax.fori_loop(0, row_tiles, place, 0)
    pl.semaphore_wait(barrier, len(peers))

    for j in range(CT):
        send(own_v.at[j], got_z.at[j], in_send.at[j], in_recv.at[j], at_cell(2))

    def weigh(t, carry):
        spot = pl.ds(pl.multiple_of(t * TILE, TILE), TILE)
        row = weight[pl.ds(t, 1), :]
        for i in range(CT):
            turned = own_v[i, spot, :].astype(jnp.float32).T
            own_wt[i * TILE : (i + 1) * TILE, spot] = (turned * row).astype(jnp.bfloat16)
        return carry

    lax.fori_loop(0, row_tiles, weigh, 0)
    send(own_wt, got_r, in_send.at[8], in_recv.at[8], r_target)

    def multiply(stage, left, pieces):
        part = stage.refs[0]

        def rows(m, carry):
            spot = pl.ds(pl.multiple_of(m * TILE, TILE), TILE)
            lhs = left[spot, :]
            for i in range(0, len(pieces), 2):
                rhs = jnp.concatenate([pieces[i][...], pieces[i + 1][...]], axis=1)
                got = jnp.dot(lhs, rhs, preferred_element_type=jnp.float32)
                part[i, spot, :] = got[:, :TILE]
                part[i + 1, spot, :] = got[:, TILE:]
            return carry

        lax.fori_loop(0, CT, rows, 0)

    def own_part(stage, dest):
        return stage.refs[0][:, pl.ds(pl.multiple_of(dest * chunk, chunk), chunk), :]

    def arrived(stage, m):
        part, sbuf, rbuf, ssem, rsem = stage.refs[:5]
        await_recv(rbuf.at[m], ssem.at[m], rsem.at[m])
        rows = stage.items * chunk
        codes = rbuf[m, 0:rows, :].astype(jnp.int32).astype(jnp.float32)
        power = rbuf[m, rows : rows + 16, :].astype(jnp.int32).astype(jnp.float32)[0:1]
        scale = jnp.exp2(power * (1.0 / STEP)) * (1.0 / FULL)
        return (codes * scale).reshape(stage.items, chunk, TILE)

    def step(stage, s):
        part, sbuf, rbuf, ssem, rsem = stage.refs[:5]
        rows = stage.items * chunk
        for path, first in zip(stage.streams, stage.first):
            if s >= len(path):
                continue
            o, m = path[s], first + s
            x = own_part(stage, lax.rem(z - o + nz, nz))
            if s > 0:
                x = x + arrived(stage, m - 1)
            codes, power = coded(x)
            sbuf[m, 0:rows, :] = codes.reshape(rows, TILE)
            sbuf[m, rows : rows + 16, :] = jnp.broadcast_to(power, (16, TILE)).astype(jnp.int32).astype(jnp.int16)
            ahead = path[s + 1] if s + 1 < len(path) else 0
            send(sbuf.at[m], rbuf.at[m], ssem.at[m], rsem.at[m], at_z(ahead - o))

    def gather(stage):
        part, sbuf, rbuf, ssem, rsem, total, other, swap = stage.refs
        x = own_part(stage, z)
        for path, first in zip(stage.streams, stage.first):
            x = x + arrived(stage, first + len(path) - 1)
        half = chunk // 2
        total[0] = x[:, :half]
        total[1] = x[:, half:]
        send(total.at[1 - yl], other, swap.at[0], swap.at[1], across)

    def finish(stage):
        part, sbuf, rbuf, ssem, rsem, total, other, swap = stage.refs
        await_recv(other, swap.at[0], swap.at[1])
        return total[yl] + other[...]

    a, b = stages[0], stages[1]
    visits = stages[2:]
    sib_s = 1 + 2 * odd
    b_s = 3 - 2 * odd

    def start_a():
        multiply(a, own_wt, [own_v.at[j] for j in range(CT)])

    def start_b():
        await_recv(got_r, in_send.at[8], in_recv.at[8])
        multiply(b, got_r, [own_v.at[j] for j in range(CT)])

    def pass_on(j):
        await_recv(got_z.at[j], in_send.at[j], in_recv.at[j])
        send(got_z.at[j], got_sib.at[j], in_send.at[4 + j], in_recv.at[4 + j], sibling)

    def start_c(j):
        await_recv(got_sib.at[j], in_send.at[4 + j], in_recv.at[4 + j])
        multiply(visits[j], own_wt, [got_z.at[j], got_sib.at[j]])

    def finish_a():
        x = finish(a)
        for i in range(CT):
            out[0, 0, :, i * TILE : (i + 1) * TILE] = x[i]

    def finish_b():
        b_out[...] = finish(b)
        send(b_out, b_in, b_send, b_recv, r_source)

    def take_b():
        await_recv(b_in, b_send, b_recv)
        for i in range(CT):
            out[b_s, 0, :, i * TILE : (i + 1) * TILE] = b_in[i]

    def finish_c(j):
        x = finish(visits[j])
        out[2, 0, :, j * TILE : (j + 1) * TILE] = x[0]
        out[sib_s, 0, :, j * TILE : (j + 1) * TILE] = x[1]

    events = []
    tick = 4.2

    def run(stage, ready, begin, end):
        events.append((ready, begin))
        for s in range(stage.steps):
            events.append((ready + 0.1 + tick * s, functools.partial(step, stage, s)))
        events.append((ready + 0.1 + tick * stage.steps, functools.partial(gather, stage)))
        events.append((ready + 3.5 + tick * stage.steps, end))

    run(a, 0.0, start_a, finish_a)
    run(b, 14.0, start_b, finish_b)
    events.append((14.0 + 7.0 + tick * b.steps, take_b))
    for j in range(CT):
        ready = 4.0 + 5.3 * (j + 1)
        events.append((ready, functools.partial(pass_on, j)))
        run(visits[j], ready + 2.0, functools.partial(start_c, j), functools.partial(finish_c, j))
    for _, event in sorted(events, key=lambda e: e[0]):
        event()
    for copy in started:
        copy.wait_send()


def body(nz, plan, tile_values, tile_cols, tile_count, ray_weight):
    row_tiles = tile_values.shape[0]
    rays = row_tiles * TILE
    chunk = CT * TILE // nz
    bf16, f32 = jnp.bfloat16, jnp.float32
    dma = pltpu.SemaphoreType.DMA
    scratch = [
        pltpu.VMEM((CT, rays, TILE), bf16),
        pltpu.VMEM((CT * TILE, rays), bf16),
        pltpu.VMEM((CT, rays, TILE), bf16),
        pltpu.VMEM((CT, rays, TILE), bf16),
        pltpu.VMEM((CT * TILE, rays), bf16),
        dma((9,)),
        dma((9,)),
    ]
    for name, items, stride, mirror in plan:
        count = nz - 1
        rows = items * chunk + 16
        scratch += [
            pltpu.VMEM((items, CT * TILE, TILE), f32),
            pltpu.VMEM((count, rows, TILE), jnp.int16),
            pltpu.VMEM((count, rows, TILE), jnp.int16),
            dma((count,)),
            dma((count,)),
            pltpu.VMEM((2, items, chunk // 2, TILE), f32),
            pltpu.VMEM((items, chunk // 2, TILE), f32),
            dma((2,)),
        ]
    scratch += [
        pltpu.VMEM((CT, chunk // 2, TILE), f32),
        pltpu.VMEM((CT, chunk // 2, TILE), f32),
        dma,
        dma,
    ]
    vmem, smem = pl.BlockSpec(memory_space=pltpu.VMEM), pl.BlockSpec(memory_space=pltpu.SMEM)
    return pl.pallas_call(
        functools.partial(kernel, nz, plan),
        out_shape=jax.ShapeDtypeStruct((4, 1, chunk // 2, CT * TILE), f32),
        in_specs=[vmem, smem, smem, vmem],
        out_specs=vmem,
        scratch_shapes=scratch,
        compiler_params=pltpu.CompilerParams(
            collective_id=0, has_side_effects=True, vmem_limit_bytes=48 << 20
        ),
    )(
        tile_values.reshape(row_tiles, K, TILE, TILE),
        tile_cols.reshape(row_tiles, K),
        tile_count.reshape(row_tiles),
        ray_weight.reshape(row_tiles, TILE),
    )


def solution(mesh):
    return jax.shard_map(
        functools.partial(body, mesh.shape["ray"] // 2, PLAN),
        mesh=mesh,
        in_specs=(P("ray", "cell", None, None, None), P("ray", "cell", None), P("ray", "cell"), P("ray")),
        out_specs=P(None, "cell", "ray", None),
        check_vma=False,
    )
```

time: 202 us -> 82.6 us (0.41)
  the two profiles are of different devices: /device:TPU:1 before, /device:TPU:2 now
where the time goes in v1:
time: 82.6 us; the launch traced here: 82.4 us
  Pallas kernels  79.2 us (96%)
  local copies, waits for them, and re-layouts  3.22 us (4%)
    pallas_call x1, Pallas kernels, body(): pl.pallas_call(functools.partial(kernel, nz, plan), out_shape=jax.ShapeDt...  79.2 us
    unnamed x9, local copies, waits for them, and re-layouts  3.14 us

profile of v1, /device:TPU:2, one launch (start us, length us, event | category | flops | bytes accessed | tf_op | source)
XLA Modules:
  0.0 82.4 jit_solution(15902663040111248777)
XLA Ops:
  0.0 0.0 copy-start.3
  0.0 0.0 copy-start.1
  0.0 0.7 copy-done.3
  0.7 0.0 copy-start.2
  0.7 0.1 copy.5.cols
  0.8 0.0 copy-done.1
  0.8 0.6 copy-done.2
  1.3 0.0 copy-start
  1.3 1.2 %copy-done = bf16[8,1,4,128,128]{4,3,2,1,0:T(8,128)(2,1)S(1)} copy-done((bf16[8,1,4,128,128]{4,3,2,1,0:T(8,128)(2,1)S(1)}, bf16[8,1,4,128,128]{4,3,2,1,0:T(8,128)(2,1)}, u32[]{:S(2)}) %copy-start) | copy-done | bytes 1048600
  2.6 79.2 %shard_map.46 = f32[4,1,16,512]{3,2,1,0:T(8,128)S(1)} custom-call(bf16[8,4,128,128]{3,2,1,0:T(8,128)(2,1)S(1)} %bitcast.4, s32[8,4]{1,0:T(8,128)S(1)} %copy.5.cols, s32[8]{0:T(128)S(1)} %bitcast.6, f32[8,128]{1,0:T(8,128)S(1)} %bitcast.5), custom_call_target="tpu_custom_call" | custom-call | tf_op jit(solution)/shard_map/pallas_call | solution.py:291
  81.8 0.7 copy.7
Async XLA Ops:
  0.0 0.7 copy-start.3
  0.0 0.8 copy-start.1
  0.7 0.7 copy-start.2
  1.3 1.2 %copy-start = (bf16[8,1,4,128,128]{4,3,2,1,0:T(8,128)(2,1)S(1)}, bf16[8,1,4,128,128]{4,3,2,1,0:T(8,128)(2,1)}, u32[]{:S(2)}) copy-start(bf16[8,1,4,128,128]{4,3,2,1,0:T(8,128)(2,1)} %param.4) | copy-start | bytes 3145732

commit v2 on v1

--- a/solution.py
+++ b/solution.py
@@ -27,18 +27,40 @@
 
 
 class Stage:
-    def __init__(self, name, items, streams, refs):
-        self.name, self.items, self.streams, self.refs = name, items, streams, refs
-        self.first = []
-        count = 0
-        for path in streams:
-            self.first.append(count)
-            count += len(path)
-        self.messages = count
-        self.steps = max(len(path) for path in streams)
-
-
-PLAN = (("a", 4, 2, False), ("b", 4, 2, True), ("c0", 2, 2, False), ("c1", 2, 2, True), ("c2", 2, 2, False), ("c3", 2, 2, True))
+    def __init__(self, items, size, stride, mirror, near_first, refs):
+        self.items, self.near_first, self.refs = items, near_first, refs
+        self.paths = streams_of(size, stride, mirror)
+        self.steps = []
+        self.place = {}
+        self.count = 0
+        self.widest = 1
+        for s in range(max(len(path) for path in self.paths)):
+            groups = {}
+            for k, path in enumerate(self.paths):
+                if s < len(path):
+                    ahead = path[s + 1] if s + 1 < len(path) else 0
+                    groups.setdefault(ahead - path[s], []).append(k)
+            found = []
+            for hop, members in groups.items():
+                for slot, k in enumerate(members):
+                    self.place[k, s] = (self.count, slot, len(members))
+                self.widest = max(self.widest, len(members))
+                found.append((self.count, hop, members))
+                self.count += 1
+            self.steps.append(found)
+        self.hops = {hop for found in self.steps for _, hop, _ in found}
+        self.seen = set()
+
+
+PLAN = (
+    ("a", 4, 1, False, False),
+    ("b", 4, 1, True, False),
+    ("c0", 2, 1, False, False),
+    ("c1", 2, 1, True, False),
+    ("c2", 2, 2, False, True),
+    ("c3", 2, 2, True, True),
+)
+TICK = {1: 3.5, 2: 4.1, 4: 5.5, 8: 9.0}
 
 
 def coded(x):
@@ -49,20 +71,21 @@
 
 
 def kernel(nz, plan, values, cols, count, weight, out, *scratch):
-    n_stages = len(plan)
-    (own_v, own_wt, got_z, got_sib, got_r, in_send, in_recv) = scratch[:7]
-    per = scratch[7 : 7 + 8 * n_stages]
-    (b_out, b_in, b_send, b_recv) = scratch[7 + 8 * n_stages :]
+    (held, in_copy, own_v, own_wt, got_z, got_sib, got_r, in_send, in_recv) = scratch[:9]
+    (b_out, b_in, b_send, b_recv) = scratch[-4:]
     stages = []
-    for i, (name, items, stride, mirror) in enumerate(plan):
-        stages.append(Stage(name, items, streams_of(nz, stride, mirror), per[8 * i : 8 * i + 8]))
-
+    for i, (name, items, stride, mirror, near_first) in enumerate(plan):
+        stages.append(Stage(items, nz, stride, mirror, near_first, scratch[9 + 8 * i : 17 + 8 * i]))
+
+    fetch = pltpu.make_async_copy(values, held, in_copy)
+    fetch.start()
     p = lax.axis_index("cell")
     ray = lax.axis_index("ray")
     n_cell = lax.axis_size("cell")
     z, yl = ray // 2, ray % 2
     odd = p % 2
     chunk = CT * TILE // nz
+    half = chunk // 2
 
     def at_cell(shift):
         return {"ray": ray, "cell": lax.rem(p + shift + n_cell, n_cell)}
@@ -78,10 +101,8 @@
 
     shifts = set()
     for stage in stages:
-        for path in stage.streams:
-            for i, o in enumerate(path):
-                d = (path[i + 1] if i + 1 < len(path) else 0) - o
-                shifts.update((d, -d))
+        for hop in stage.hops:
+            shifts.update((hop, -hop))
     peers = [sibling, at_cell(2), at_cell(-2), third, across] + [at_z(d) for d in sorted(shifts)]
     barrier = pltpu.get_barrier_semaphore()
     for peer in peers:
@@ -106,16 +127,17 @@
     def placed(t, i):
         slot, live = jnp.int32(0), jnp.int32(0)
         for k in range(K):
-            here = jnp.where((cols[t, k] == i) & (k < count[t]), 1, 0)
+            here = jnp.where((cols[k, t] == i) & (k < count[t]), 1, 0)
             slot += k * here
             live += here
-        return values[t, slot].astype(jnp.float32) * live.astype(jnp.float32)
+        return held[t, slot].astype(jnp.float32) * live.astype(jnp.float32)
 
     def place(t, carry):
         for i in range(CT):
             own_v[i, pl.ds(pl.multiple_of(t * TILE, TILE), TILE), :] = placed(t, i).astype(jnp.bfloat16)
         return carry
 
+    fetch.wait()
     lax.fori_loop(0, row_tiles, place, 0)
     pl.semaphore_wait(barrier, len(peers))
 
@@ -142,52 +164,92 @@
             for i in range(0, len(pieces), 2):
                 rhs = jnp.concatenate([pieces[i][...], pieces[i + 1][...]], axis=1)
                 got = jnp.dot(lhs, rhs, preferred_element_type=jnp.float32)
-                part[i, spot, :] = got[:, :TILE]
-                part[i + 1, spot, :] = got[:, TILE:]
+                for e in (0, 1):
+                    tile = got[:, e * TILE : (e + 1) * TILE]
+                    if not stage.near_first:
+                        part[0, i + e, spot, :] = tile
+                        continue
+                    for q in range(TILE // half):
+                        to = pl.ds(pl.multiple_of(m * (TILE // 2) + q // 2 * half, half), half)
+                        part[q % 2, i + e, to, :] = tile[q * half : (q + 1) * half]
             return carry
 
         lax.fori_loop(0, CT, rows, 0)
 
+    def decoded(buf, m, slot, width, rows):
+        first = 16 + slot * rows
+        codes = buf[m, first : first + rows, :].astype(jnp.int32).astype(jnp.float32)
+        power = buf[m, 0:16, :].astype(jnp.int32).astype(jnp.float32)
+        at = slot * (16 // width)
+        return codes * (jnp.exp2(power[at : at + 1] * (1.0 / STEP)) * (1.0 / FULL))
+
+    def encode(buf, m, pieces):
+        lines = lax.broadcasted_iota(jnp.int32, (16, TILE), 0)
+        for slot, x in enumerate(pieces):
+            codes, power = coded(x)
+            rows = x.shape[0] * x.shape[1]
+            buf[m, 16 + slot * rows : 16 + (slot + 1) * rows, :] = codes.reshape(rows, TILE)
+            power = jnp.broadcast_to(power, (16, TILE))
+            powers = power if slot == 0 else jnp.where(lines >= slot * (16 // len(pieces)), power, powers)
+        buf[m, 0:16, :] = powers.astype(jnp.int32).astype(jnp.int16)
+
     def own_part(stage, dest):
-        return stage.refs[0][:, pl.ds(pl.multiple_of(dest * chunk, chunk), chunk), :]
-
-    def arrived(stage, m):
+        part = stage.refs[0]
+        if stage.near_first:
+            return part[yl, :, pl.ds(pl.multiple_of(dest * half, half), half), :]
+        return part[0, :, pl.ds(pl.multiple_of(dest * chunk, chunk), chunk), :]
+
+    def arrived(stage, k, s):
         part, sbuf, rbuf, ssem, rsem = stage.refs[:5]
-        await_recv(rbuf.at[m], ssem.at[m], rsem.at[m])
-        rows = stage.items * chunk
-        codes = rbuf[m, 0:rows, :].astype(jnp.int32).astype(jnp.float32)
-        power = rbuf[m, rows : rows + 16, :].astype(jnp.int32).astype(jnp.float32)[0:1]
-        scale = jnp.exp2(power * (1.0 / STEP)) * (1.0 / FULL)
-        return (codes * scale).reshape(stage.items, chunk, TILE)
+        m, slot, width = stage.place[k, s]
+        tall = half if stage.near_first else chunk
+        rows = stage.items * tall
+        if m not in stage.seen:
+            stage.seen.add(m)
+            spot = rbuf.at[m, pl.ds(0, 16 + width * rows)]
+            await_recv(spot, ssem.at[m], rsem.at[m])
+        return decoded(rbuf, m, slot, width, rows).reshape(stage.items, tall, TILE)
 
     def step(stage, s):
         part, sbuf, rbuf, ssem, rsem = stage.refs[:5]
-        rows = stage.items * chunk
-        for path, first in zip(stage.streams, stage.first):
-            if s >= len(path):
-                continue
-            o, m = path[s], first + s
-            x = own_part(stage, lax.rem(z - o + nz, nz))
-            if s > 0:
-                x = x + arrived(stage, m - 1)
-            codes, power = coded(x)
-            sbuf[m, 0:rows, :] = codes.reshape(rows, TILE)
-            sbuf[m, rows : rows + 16, :] = jnp.broadcast_to(power, (16, TILE)).astype(jnp.int32).astype(jnp.int16)
-            ahead = path[s + 1] if s + 1 < len(path) else 0
-            send(sbuf.at[m], rbuf.at[m], ssem.at[m], rsem.at[m], at_z(ahead - o))
+        for m, hop, members in stage.steps[s]:
+            pieces = []
+            for k in members:
+                x = own_part(stage, lax.rem(z - stage.paths[k][s] + nz, nz))
+                pieces.append(x if s == 0 else x + arrived(stage, k, s - 1))
+            encode(sbuf, m, pieces)
+            size = 16 + len(members) * pieces[0].shape[0] * pieces[0].shape[1]
+            spot = pl.ds(0, size)
+            send(sbuf.at[m, spot], rbuf.at[m, spot], ssem.at[m], rsem.at[m], at_z(hop))
+
+    def summed(stage):
+        x = own_part(stage, z)
+        for k, path in enumerate(stage.paths):
+            x = x + arrived(stage, k, len(path) - 1)
+        return x
+
+    def cross(stage):
+        part, near_out, near_in, swap = stage.refs[0], stage.refs[5], stage.refs[6], stage.refs[7]
+        encode(near_out, 0, [part[1 - yl]])
+        send(near_out, near_in, swap.at[0], swap.at[1], across)
+
+    def merge(stage):
+        part, near_in, swap = stage.refs[0], stage.refs[6], stage.refs[7]
+        await_recv(near_in, swap.at[0], swap.at[1])
+        rows = stage.items * half * nz
+        part[yl] = part[yl] + decoded(near_in, 0, 0, 1, rows).reshape(stage.items, half * nz, TILE)
 
     def gather(stage):
-        part, sbuf, rbuf, ssem, rsem, total, other, swap = stage.refs
-        x = own_part(stage, z)
-        for path, first in zip(stage.streams, stage.first):
-            x = x + arrived(stage, first + len(path) - 1)
-        half = chunk // 2
+        total, other, swap = stage.refs[5:]
+        x = summed(stage)
         total[0] = x[:, :half]
         total[1] = x[:, half:]
         send(total.at[1 - yl], other, swap.at[0], swap.at[1], across)
 
     def finish(stage):
-        part, sbuf, rbuf, ssem, rsem, total, other, swap = stage.refs
+        if stage.near_first:
+            return summed(stage)
+        total, other, swap = stage.refs[5:]
         await_recv(other, swap.at[0], swap.at[1])
         return total[yl] + other[...]
 
@@ -231,22 +293,30 @@
         out[sib_s, 0, :, j * TILE : (j + 1) * TILE] = x[1]
 
     events = []
-    tick = 4.2
-
-    def run(stage, ready, begin, end):
+
+    def run(stage, stride, ready, begin, end):
         events.append((ready, begin))
-        for s in range(stage.steps):
+        tick = TICK[stride]
+        if stage.near_first:
+            events.append((ready + 0.01, functools.partial(cross, stage)))
+            events.append((ready + 4.5, functools.partial(merge, stage)))
+            ready += 4.5
+        for s in range(len(stage.steps)):
             events.append((ready + 0.1 + tick * s, functools.partial(step, stage, s)))
-        events.append((ready + 0.1 + tick * stage.steps, functools.partial(gather, stage)))
-        events.append((ready + 3.5 + tick * stage.steps, end))
-
-    run(a, 0.0, start_a, finish_a)
-    run(b, 14.0, start_b, finish_b)
-    events.append((14.0 + 7.0 + tick * b.steps, take_b))
+        ready += 0.1 + tick * len(stage.steps)
+        if not stage.near_first:
+            events.append((ready, functools.partial(gather, stage)))
+            ready += 3.4
+        events.append((ready, end))
+        return ready
+
+    run(a, plan[0][2], 0.0, start_a, finish_a)
+    done = run(b, plan[1][2], 14.0, start_b, finish_b)
+    events.append((done + 3.4, take_b))
     for j in range(CT):
-        ready = 4.0 + 5.3 * (j + 1)
+        ready = 3.0 + 5.1 * (j + 1)
         events.append((ready, functools.partial(pass_on, j)))
-        run(visits[j], ready + 2.0, functools.partial(start_c, j), functools.partial(finish_c, j))
+        run(visits[j], plan[2 + j][2], ready + 1.7, functools.partial(start_c, j), functools.partial(finish_c, j))
     for _, event in sorted(events, key=lambda e: e[0]):
         event()
     for copy in started:
@@ -260,6 +330,8 @@
     bf16, f32 = jnp.bfloat16, jnp.float32
     dma = pltpu.SemaphoreType.DMA
     scratch = [
+        pltpu.VMEM((row_tiles, K, TILE, TILE), bf16),
+        dma,
         pltpu.VMEM((CT, rays, TILE), bf16),
         pltpu.VMEM((CT * TILE, rays), bf16),
         pltpu.VMEM((CT, rays, TILE), bf16),
@@ -268,17 +340,19 @@
         dma((9,)),
         dma((9,)),
     ]
-    for name, items, stride, mirror in plan:
-        count = nz - 1
-        rows = items * chunk + 16
+    half = chunk // 2
+    for name, items, stride, mirror, near_first in plan:
+        stage = Stage(items, nz, stride, mirror, near_first, None)
+        rows = 16 + stage.widest * items * (half if near_first else chunk)
+        near = (1, 16 + items * half * nz, TILE)
         scratch += [
-            pltpu.VMEM((items, CT * TILE, TILE), f32),
-            pltpu.VMEM((count, rows, TILE), jnp.int16),
-            pltpu.VMEM((count, rows, TILE), jnp.int16),
-            dma((count,)),
-            dma((count,)),
-            pltpu.VMEM((2, items, chunk // 2, TILE), f32),
-            pltpu.VMEM((items, chunk // 2, TILE), f32),
+            pltpu.VMEM((2, items, half * nz, TILE) if near_first else (1, items, chunk * nz, TILE), f32),
+            pltpu.VMEM((stage.count, rows, TILE), jnp.int16),
+            pltpu.VMEM((stage.count, rows, TILE), jnp.int16),
+            dma((stage.count,)),
+            dma((stage.count,)),
+            pltpu.VMEM(near, jnp.int16) if near_first else pltpu.VMEM((2, items, half, TILE), f32),
+            pltpu.VMEM(near, jnp.int16) if near_first else pltpu.VMEM((items, half, TILE), f32),
             dma((2,)),
         ]
     scratch += [
@@ -291,15 +365,15 @@
     return pl.pallas_call(
         functools.partial(kernel, nz, plan),
         out_shape=jax.ShapeDtypeStruct((4, 1, chunk // 2, CT * TILE), f32),
-        in_specs=[vmem, smem, smem, vmem],
+        in_specs=[pl.BlockSpec(memory_space=pltpu.HBM), smem, smem, vmem],
         out_specs=vmem,
         scratch_shapes=scratch,
         compiler_params=pltpu.CompilerParams(
-            collective_id=0, has_side_effects=True, vmem_limit_bytes=48 << 20
+            collective_id=0, has_side_effects=True, vmem_limit_bytes=62 << 20
         ),
     )(
         tile_values.reshape(row_tiles, K, TILE, TILE),
-        tile_cols.reshape(row_tiles, K),
+        tile_cols.reshape(row_tiles, K).T,
         tile_count.reshape(row_tiles),
         ray_weight.reshape(row_tiles, TILE),
     )

time: 82.6 us -> 71.2 us (0.86)
  the two profiles are of different devices: /device:TPU:2 before, /device:TPU:1 now
where the time goes in v2:
time: 71.2 us; the launch traced here: 71 us
  Pallas kernels  69.4 us (97%)
  local copies, waits for them, and re-layouts  1.57 us (2%)
    pallas_call x1, Pallas kernels, body(): pl.pallas_call(functools.partial(kernel, nz, plan), out_shape=jax.ShapeDt...  69.4 us
    unnamed x1, local copies, waits for them, and re-layouts  1.57 us

profile of v2, /device:TPU:1, one launch (start us, length us, event | category | flops | bytes accessed | tf_op | source)
XLA Modules:
  0.0 71.0 jit_solution(10029797094320109613)
XLA Ops:
  0.0 69.4 %shard_map.46 = f32[4,1,16,512]{3,2,1,0:T(8,128)} custom-call(bf16[8,4,128,128]{3,2,1,0:T(8,128)(2,1)} %bitcast.6, s32[4,8]{1,0:T(4,128)} %bitcast.8, s32[8]{0:T(128)} %bitcast.9, f32[8,128]{1,0:T(8,128)} %bitcast.7), custom_call_target="tpu_custom_call" | custom-call | tf_op jit(solution)/shard_map/pallas_call | solution.py:365
  69.4 1.6 %copy.6 = f32[4,1,16,512]{3,2,1,0:T(8,128)} copy(f32[4,1,16,512]{3,2,1,0:T(8,128)} %shard_map.46) | data formatting | bytes 262144

commit v3 on v2

--- a/solution.py
+++ b/solution.py
@@ -52,14 +52,8 @@
         self.seen = set()
 
 
-PLAN = (
-    ("a", 4, 1, False, False),
-    ("b", 4, 1, True, False),
-    ("c0", 2, 1, False, False),
-    ("c1", 2, 1, True, False),
-    ("c2", 2, 2, False, True),
-    ("c3", 2, 2, True, True),
-)
+PLAN = (('a', 4, 1, False, False), ('b0', 4, 1, True, False), ('b1', 4, 2, True, False), ('c0', 2, 1, False, False), ('c1', 2, 1, True, False), ('c2', 2, 2, False, True), ('c3', 2, 2, True, True))
+B_READY = (5.0, 14.0)
 TICK = {1: 3.5, 2: 4.1, 4: 5.5, 8: 9.0}
 
 
@@ -86,6 +80,7 @@
     odd = p % 2
     chunk = CT * TILE // nz
     half = chunk // 2
+    far = 1 - yl
 
     def at_cell(shift):
         return {"ray": ray, "cell": lax.rem(p + shift + n_cell, n_cell)}
@@ -109,15 +104,16 @@
         pl.semaphore_signal(barrier, inc=1, device_id=peer, device_id_type=MESH)
 
     row_tiles = values.shape[0]
-    started = []
-
-    def send(src, dst, ssem, rsem, to):
+    started = {}
+    guard = [None]
+
+    def send(ends, to):
+        src, dst, ssem, rsem = ends()
         copy = pltpu.make_async_remote_copy(
             src_ref=src, dst_ref=dst, send_sem=ssem, recv_sem=rsem, device_id=to, device_id_type=MESH
         )
         copy.start()
-        started.append(copy)
-        return copy
+        started.setdefault(guard[0], []).append(ends)
 
     def await_recv(dst, ssem, rsem):
         pltpu.make_async_remote_copy(
@@ -142,7 +138,7 @@
     pl.semaphore_wait(barrier, len(peers))
 
     for j in range(CT):
-        send(own_v.at[j], got_z.at[j], in_send.at[j], in_recv.at[j], at_cell(2))
+        send(lambda j=j: (own_v.at[j], got_z.at[j], in_send.at[j], in_recv.at[j]), at_cell(2))
 
     def weigh(t, carry):
         spot = pl.ds(pl.multiple_of(t * TILE, TILE), TILE)
@@ -153,7 +149,7 @@
         return carry
 
     lax.fori_loop(0, row_tiles, weigh, 0)
-    send(own_wt, got_r, in_send.at[8], in_recv.at[8], r_target)
+    send(lambda: (own_wt, got_r, in_send.at[8], in_recv.at[8]), r_target)
 
     def multiply(stage, left, pieces):
         part = stage.refs[0]
@@ -219,8 +215,12 @@
                 pieces.append(x if s == 0 else x + arrived(stage, k, s - 1))
             encode(sbuf, m, pieces)
             size = 16 + len(members) * pieces[0].shape[0] * pieces[0].shape[1]
-            spot = pl.ds(0, size)
-            send(sbuf.at[m, spot], rbuf.at[m, spot], ssem.at[m], rsem.at[m], at_z(hop))
+
+            def ends(m=m, size=size):
+                spot = pl.ds(0, size)
+                return sbuf.at[m, spot], rbuf.at[m, spot], ssem.at[m], rsem.at[m]
+
+            send(ends, at_z(hop))
 
     def summed(stage):
         x = own_part(stage, z)
@@ -230,8 +230,8 @@
 
     def cross(stage):
         part, near_out, near_in, swap = stage.refs[0], stage.refs[5], stage.refs[6], stage.refs[7]
-        encode(near_out, 0, [part[1 - yl]])
-        send(near_out, near_in, swap.at[0], swap.at[1], across)
+        encode(near_out, 0, [part[far]])
+        send(lambda: (near_out, near_in, swap.at[0], swap.at[1]), across)
 
     def merge(stage):
         part, near_in, swap = stage.refs[0], stage.refs[6], stage.refs[7]
@@ -244,7 +244,7 @@
         x = summed(stage)
         total[0] = x[:, :half]
         total[1] = x[:, half:]
-        send(total.at[1 - yl], other, swap.at[0], swap.at[1], across)
+        send(lambda: (total.at[far], other, swap.at[0], swap.at[1]), across)
 
     def finish(stage):
         if stage.near_first:
@@ -253,21 +253,29 @@
         await_recv(other, swap.at[0], swap.at[1])
         return total[yl] + other[...]
 
-    a, b = stages[0], stages[1]
-    visits = stages[2:]
+    a, b0, b1 = stages[:3]
+    visits = stages[3:]
     sib_s = 1 + 2 * odd
     b_s = 3 - 2 * odd
 
     def start_a():
         multiply(a, own_wt, [own_v.at[j] for j in range(CT)])
 
-    def start_b():
+    def only(parity, do):
+        def guarded():
+            guard[0] = parity
+            pl.when(odd == parity)(do)
+            guard[0] = None
+
+        return guarded
+
+    def start_b(b):
         await_recv(got_r, in_send.at[8], in_recv.at[8])
         multiply(b, got_r, [own_v.at[j] for j in range(CT)])
 
     def pass_on(j):
         await_recv(got_z.at[j], in_send.at[j], in_recv.at[j])
-        send(got_z.at[j], got_sib.at[j], in_send.at[4 + j], in_recv.at[4 + j], sibling)
+        send(lambda: (got_z.at[j], got_sib.at[j], in_send.at[4 + j], in_recv.at[4 + j]), sibling)
 
     def start_c(j):
         await_recv(got_sib.at[j], in_send.at[4 + j], in_recv.at[4 + j])
@@ -278,9 +286,9 @@
         for i in range(CT):
             out[0, 0, :, i * TILE : (i + 1) * TILE] = x[i]
 
-    def finish_b():
+    def finish_b(b):
         b_out[...] = finish(b)
-        send(b_out, b_in, b_send, b_recv, r_source)
+        send(lambda: (b_out, b_in, b_send, b_recv), r_source)
 
     def take_b():
         await_recv(b_in, b_send, b_recv)
@@ -294,33 +302,47 @@
 
     events = []
 
-    def run(stage, stride, ready, begin, end):
-        events.append((ready, begin))
+    def run(stage, stride, ready, begin, end, parity=None):
+        def add(time, event):
+            events.append((time, event if parity is None else only(parity, event)))
+
+        add(ready, begin)
         tick = TICK[stride]
         if stage.near_first:
-            events.append((ready + 0.01, functools.partial(cross, stage)))
-            events.append((ready + 4.5, functools.partial(merge, stage)))
+            add(ready + 0.01, functools.partial(cross, stage))
+            add(ready + 4.5, functools.partial(merge, stage))
             ready += 4.5
         for s in range(len(stage.steps)):
-            events.append((ready + 0.1 + tick * s, functools.partial(step, stage, s)))
+            add(ready + 0.1 + tick * s, functools.partial(step, stage, s))
         ready += 0.1 + tick * len(stage.steps)
         if not stage.near_first:
-            events.append((ready, functools.partial(gather, stage)))
+            add(ready, functools.partial(gather, stage))
             ready += 3.4
-        events.append((ready, end))
+        add(ready, end)
         return ready
 
     run(a, plan[0][2], 0.0, start_a, finish_a)
-    done = run(b, plan[1][2], 14.0, start_b, finish_b)
+    run(b0, plan[1][2], B_READY[0], functools.partial(start_b, b0), functools.partial(finish_b, b0), 0)
+    done = run(b1, plan[2][2], B_READY[1], functools.partial(start_b, b1), functools.partial(finish_b, b1), 1)
     events.append((done + 3.4, take_b))
     for j in range(CT):
         ready = 3.0 + 5.1 * (j + 1)
         events.append((ready, functools.partial(pass_on, j)))
-        run(visits[j], plan[2 + j][2], ready + 1.7, functools.partial(start_c, j), functools.partial(finish_c, j))
+        run(visits[j], plan[3 + j][2], ready + 1.7, functools.partial(start_c, j), functools.partial(finish_c, j))
     for _, event in sorted(events, key=lambda e: e[0]):
         event()
-    for copy in started:
-        copy.wait_send()
+    def drain(copies):
+        for ends in copies:
+            src, dst, ssem, rsem = ends()
+            pltpu.make_async_remote_copy(
+                src_ref=src, dst_ref=dst, send_sem=ssem, recv_sem=rsem, device_id=sibling, device_id_type=MESH
+            ).wait_send()
+
+    for parity, copies in started.items():
+        if parity is None:
+            drain(copies)
+        else:
+            pl.when(odd == parity)(functools.partial(drain, copies))
 
 
 def body(nz, plan, tile_values, tile_cols, tile_count, ray_weight):

time: 71.2 us -> 68.4 us (0.961); the launches traced: 71 us -> 67.5 us
  Pallas kernels: 69.4 us -> 65.9 us
    pallas_call x1, Pallas kernels: 69.4 us -> 65.9 us  [body(): pl.pallas_call(functools.partial(kernel, nz, plan), out_shape=jax.ShapeDt...]
where the time goes in v3:
time: 68.4 us; the launch traced here: 67.5 us
  Pallas kernels  65.9 us (96%)
  local copies, waits for them, and re-layouts  1.57 us (2%)
    pallas_call x1, Pallas kernels, body(): pl.pallas_call(functools.partial(kernel, nz, plan), out_shape=jax.ShapeDt...  65.9 us
    unnamed x1, local copies, waits for them, and re-layouts  1.57 us

profile of v3, /device:TPU:1, one launch (start us, length us, event | category | flops | bytes accessed | tf_op | source)
XLA Modules:
  0.0 67.5 jit_solution(4325489975860302145)
XLA Ops:
  0.0 65.9 %shard_map.46 = f32[4,1,16,512]{3,2,1,0:T(8,128)} custom-call(bf16[8,4,128,128]{3,2,1,0:T(8,128)(2,1)} %bitcast.6, s32[4,8]{1,0:T(4,128)} %bitcast.8, s32[8]{0:T(128)} %bitcast.9, f32[8,128]{1,0:T(8,128)} %bitcast.7), custom_call_target="tpu_custom_call" | custom-call | tf_op jit(solution)/shard_map/pallas_call | solution.py:387
  65.9 1.6 %copy.6 = f32[4,1,16,512]{3,2,1,0:T(8,128)} copy(f32[4,1,16,512]{3,2,1,0:T(8,128)} %shard_map.46) | data formatting | bytes 262144

commit v4 on v3

--- a/solution.py
+++ b/solution.py
@@ -52,9 +52,24 @@
         self.seen = set()
 
 
-PLAN = (('a', 4, 1, False, False), ('b0', 4, 1, True, False), ('b1', 4, 2, True, False), ('c0', 2, 1, False, False), ('c1', 2, 1, True, False), ('c2', 2, 2, False, True), ('c3', 2, 2, True, True))
-B_READY = (5.0, 14.0)
-TICK = {1: 3.5, 2: 4.1, 4: 5.5, 8: 9.0}
+PLAN = (
+    ('a', 4, 1, False, False),
+    ('b0', 4, 1, True, False),
+    ('b1', 4, 2, True, False),
+    ('c0', 2, 1, False, False),
+    ('c1', 2, 2, True, False),
+    ('c2', 2, 2, False, True),
+    ('c3', 2, 2, True, True),
+)
+ORDER = (
+    "a.begin", "a.s0", "b0.begin", "b0.s0", "pass0", "a.s1", "b0.s1", "c0.begin", "c0.s0", "a.s2", "pass1",
+    "c0.s1", "b0.s2", "c1.begin", "c1.s0", "b1.begin", "c0.s2", "a.s3", "b0.s3", "pass2", "b1.s0", "c1.s1",
+    "c2.begin", "c2.cross", "a.s4", "c0.s3", "b0.s4", "pass3", "b1.s1", "c1.s2", "c3.begin", "c3.cross",
+    "b0.s5", "c2.merge", "c0.s4", "c2.s0", "b1.s2", "b0.s6", "c3.merge", "c3.s0", "c0.s5", "a.s5", "c2.s1",
+    "b1.s3", "c0.s6", "c3.s1", "b0.s7", "a.s6", "c2.s2", "b1.gather", "c1.s3", "c0.s7", "a.s7", "b0.gather",
+    "c3.s2", "b1.end", "c2.s3", "a.gather", "b0.end", "c0.gather", "c1.gather", "c3.s3", "a.end", "takeb",
+    "c2.end", "c1.end", "c0.end", "c3.end",
+)
 
 
 def coded(x):
@@ -300,37 +315,31 @@
         out[2, 0, :, j * TILE : (j + 1) * TILE] = x[0]
         out[sib_s, 0, :, j * TILE : (j + 1) * TILE] = x[1]
 
-    events = []
-
-    def run(stage, stride, ready, begin, end, parity=None):
-        def add(time, event):
-            events.append((time, event if parity is None else only(parity, event)))
-
-        add(ready, begin)
-        tick = TICK[stride]
+    events = {}
+
+    def add(name, stage, begin, end, parity=None):
+        found = {"begin": begin, "end": end}
         if stage.near_first:
-            add(ready + 0.01, functools.partial(cross, stage))
-            add(ready + 4.5, functools.partial(merge, stage))
-            ready += 4.5
+            found["cross"] = functools.partial(cross, stage)
+            found["merge"] = functools.partial(merge, stage)
+        else:
+            found["gather"] = functools.partial(gather, stage)
         for s in range(len(stage.steps)):
-            add(ready + 0.1 + tick * s, functools.partial(step, stage, s))
-        ready += 0.1 + tick * len(stage.steps)
-        if not stage.near_first:
-            add(ready, functools.partial(gather, stage))
-            ready += 3.4
-        add(ready, end)
-        return ready
-
-    run(a, plan[0][2], 0.0, start_a, finish_a)
-    run(b0, plan[1][2], B_READY[0], functools.partial(start_b, b0), functools.partial(finish_b, b0), 0)
-    done = run(b1, plan[2][2], B_READY[1], functools.partial(start_b, b1), functools.partial(finish_b, b1), 1)
-    events.append((done + 3.4, take_b))
+            found[f"s{s}"] = functools.partial(step, stage, s)
+        for key, event in found.items():
+            events[f"{name}.{key}"] = event if parity is None else only(parity, event)
+
+    add("a", a, start_a, finish_a)
+    add("b0", b0, functools.partial(start_b, b0), functools.partial(finish_b, b0), 0)
+    add("b1", b1, functools.partial(start_b, b1), functools.partial(finish_b, b1), 1)
+    events["takeb"] = take_b
     for j in range(CT):
-        ready = 3.0 + 5.1 * (j + 1)
-        events.append((ready, functools.partial(pass_on, j)))
-        run(visits[j], plan[3 + j][2], ready + 1.7, functools.partial(start_c, j), functools.partial(finish_c, j))
-    for _, event in sorted(events, key=lambda e: e[0]):
-        event()
+        events[f"pass{j}"] = functools.partial(pass_on, j)
+        add(f"c{j}", visits[j], functools.partial(start_c, j), functools.partial(finish_c, j))
+    for name in ORDER:
+        events.pop(name)()
+    assert not events
+
     def drain(copies):
         for ends in copies:
             src, dst, ssem, rsem = ends()
@@ -391,7 +400,7 @@
         out_specs=vmem,
         scratch_shapes=scratch,
         compiler_params=pltpu.CompilerParams(
-            collective_id=0, has_side_effects=True, vmem_limit_bytes=62 << 20
+            collective_id=0, has_side_effects=True, vmem_limit_bytes=54144 << 10
         ),
     )(
         tile_values.reshape(row_tiles, K, TILE, TILE),

time: 68.4 us -> 67 us (0.980)
  the two profiles are of different devices: /device:TPU:1 before, /device:TPU:32 now
where the time goes in v4:
time: 67 us; the launch traced here: 66.8 us
  Pallas kernels  65.5 us (98%)
  local copies, waits for them, and re-layouts  1.35 us (2%)
    pallas_call x1, Pallas kernels, body(): pl.pallas_call(functools.partial(kernel, nz, plan), out_shape=jax.ShapeDt...  65.5 us
    unnamed x7, local copies, waits for them, and re-layouts  1.35 us

profile of v4, /device:TPU:32, one launch (start us, length us, event | category | flops | bytes accessed | tf_op | source)
XLA Modules:
  0.0 66.8 jit_solution(5315231443719810125)
XLA Ops:
  0.0 0.0 copy-start
  0.0 0.0 copy-start.1
  0.0 0.0 copy-start.2
  0.0 0.7 %copy-done = f32[1024]{0:T(1024)S(1)} copy-done((f32[1024]{0:T(1024)S(1)}, f32[1024]{0:T(1024)}, u32[]{:S(2)}) %copy-start) | copy-done | bytes 4120
  0.7 0.0 copy-done.1
  0.7 0.0 copy-done.2
  0.7 65.5 %shard_map.46 = f32[4,1,16,512]{3,2,1,0:T(8,128)S(1)} custom-call(bf16[8,4,128,128]{3,2,1,0:T(8,128)(2,1)} %bitcast.9, s32[4,8]{1,0:T(4,128)S(1)} %bitcast.7, s32[8]{0:T(128)S(1)} %bitcast.8, f32[8,128]{1,0:T(8,128)S(1)} %bitcast.6), custom_call_target="tpu_custom_call" | custom-call | tf_op jit(solution)/shard_map/pallas_call | solution.py:396
  66.2 0.7 copy.6
Async XLA Ops:
  0.0 0.7 %copy-start = (f32[1024]{0:T(1024)S(1)}, f32[1024]{0:T(1024)}, u32[]{:S(2)}) copy-start(f32[1024]{0:T(1024)} %param.7) | copy-start | bytes 12292
  0.0 0.7 %copy-start.1 = (s32[8,1,4]{0,2,1:T(4,128)S(1)}, s32[8,1,4]{0,2,1:T(4,128)}, u32[]{:S(2)}) copy-start(s32[8,1,4]{0,2,1:T(4,128)} %param.5) | copy-start | bytes 388
  0.0 0.7 %copy-start.2 = (s32[8,1]{0,1:T(1,128)S(1)}, s32[8,1]{0,1:T(1,128)}, u32[]{:S(2)}) copy-start(s32[8,1]{0,1:T(1,128)} %param.6) | copy-start | bytes 100

commit v5 on v4

--- a/solution.py
+++ b/solution.py
@@ -32,44 +32,51 @@
         self.paths = streams_of(size, stride, mirror)
         self.steps = []
         self.place = {}
-        self.count = 0
-        self.widest = 1
+        self.count = [0, 0]
+        self.widest = [1, 1]
         for s in range(max(len(path) for path in self.paths)):
             groups = {}
             for k, path in enumerate(self.paths):
                 if s < len(path):
-                    ahead = path[s + 1] if s + 1 < len(path) else 0
-                    groups.setdefault(ahead - path[s], []).append(k)
+                    last = s + 1 == len(path)
+                    ahead = 0 if last else path[s + 1]
+                    groups.setdefault((ahead - path[s], last and not near_first), []).append(k)
             found = []
-            for hop, members in groups.items():
+            for (hop, split), members in groups.items():
+                kind = int(split)
                 for slot, k in enumerate(members):
-                    self.place[k, s] = (self.count, slot, len(members))
-                self.widest = max(self.widest, len(members))
-                found.append((self.count, hop, members))
-                self.count += 1
+                    self.place[k, s] = (self.count[kind], slot, len(members))
+                self.widest[kind] = max(self.widest[kind], len(members))
+                found.append((self.count[kind], hop, members, split))
+                self.count[kind] += 1
             self.steps.append(found)
-        self.hops = {hop for found in self.steps for _, hop, _ in found}
+        self.hops = {hop for found in self.steps for _, hop, _, _ in found}
+        self.split_hops = {hop for found in self.steps for _, hop, _, split in found if split}
         self.seen = set()
 
 
 PLAN = (
-    ('a', 4, 1, False, False),
-    ('b0', 4, 1, True, False),
-    ('b1', 4, 2, True, False),
-    ('c0', 2, 1, False, False),
-    ('c1', 2, 2, True, False),
-    ('c2', 2, 2, False, True),
-    ('c3', 2, 2, True, True),
+    (None, 1, False, False),
+    (None, 1, True, False),
+    (None, 2, True, False),
+    ((0,), 1, False, False),
+    ((1,), 2, True, False),
+    ((2,), 2, False, True),
+    ((3,), 2, True, True),
 )
 ORDER = (
-    "a.begin", "a.s0", "b0.begin", "b0.s0", "pass0", "a.s1", "b0.s1", "c0.begin", "c0.s0", "a.s2", "pass1",
-    "c0.s1", "b0.s2", "c1.begin", "c1.s0", "b1.begin", "c0.s2", "a.s3", "b0.s3", "pass2", "b1.s0", "c1.s1",
-    "c2.begin", "c2.cross", "a.s4", "c0.s3", "b0.s4", "pass3", "b1.s1", "c1.s2", "c3.begin", "c3.cross",
-    "b0.s5", "c2.merge", "c0.s4", "c2.s0", "b1.s2", "b0.s6", "c3.merge", "c3.s0", "c0.s5", "a.s5", "c2.s1",
-    "b1.s3", "c0.s6", "c3.s1", "b0.s7", "a.s6", "c2.s2", "b1.gather", "c1.s3", "c0.s7", "a.s7", "b0.gather",
-    "c3.s2", "b1.end", "c2.s3", "a.gather", "b0.end", "c0.gather", "c1.gather", "c3.s3", "a.end", "takeb",
-    "c2.end", "c1.end", "c0.end", "c3.end",
+    "a.begin", "a.s0", "b0.begin", "b0.s0", "a.lend", "a.s1", "b0.lend", "pass0", "a.s2", "c0.begin", "c0.s0",
+    "c0.lend", "b0.s1", "a.s3", "pass1", "b0.s2", "b1.begin", "b1.s0", "c0.s1", "c1.begin", "c1.s0", "b0.s3",
+    "c0.s2", "c1.lend", "b1.lend", "pass2", "b1.s1", "c1.s1", "a.s4", "c2.begin", "c2.cross", "c0.s3",
+    "pass3", "b0.s4", "b1.s2", "c3.begin", "c3.cross", "a.s5", "b0.s5", "c2.merge", "c0.s4", "c2.s0", "b1.s3",
+    "c3.merge", "c3.s0", "b0.s6", "c0.s5", "c2.s1", "c1.s2", "c3.s1", "c2.s2", "b0.s7", "c0.s6", "b1.end",
+    "a.s6", "c3.s2", "c0.s7", "c1.s3", "c2.s3", "a.s7", "b0.end", "c3.s3", "takeb", "c0.end", "c1.end",
+    "a.end", "c2.end", "c3.end",
 )
+
+
+def items_of(tiles):
+    return CT if tiles is None else 2 * len(tiles)
 
 
 def coded(x):
@@ -83,8 +90,9 @@
     (held, in_copy, own_v, own_wt, got_z, got_sib, got_r, in_send, in_recv) = scratch[:9]
     (b_out, b_in, b_send, b_recv) = scratch[-4:]
     stages = []
-    for i, (name, items, stride, mirror, near_first) in enumerate(plan):
-        stages.append(Stage(items, nz, stride, mirror, near_first, scratch[9 + 8 * i : 17 + 8 * i]))
+    for i, (tiles, stride, mirror, near_first) in enumerate(plan):
+        refs = scratch[9 + 12 * i : 21 + 12 * i]
+        stages.append(Stage(items_of(tiles), nz, stride, mirror, near_first, refs))
 
     fetch = pltpu.make_async_copy(values, held, in_copy)
     fetch.start()
@@ -100,8 +108,8 @@
     def at_cell(shift):
         return {"ray": ray, "cell": lax.rem(p + shift + n_cell, n_cell)}
 
-    def at_z(shift):
-        return {"ray": lax.rem(z + shift + nz, nz) * 2 + yl, "cell": p}
+    def at_z(shift, h):
+        return {"ray": lax.rem(z + shift + nz, nz) * 2 + h, "cell": p}
 
     sibling = {"ray": ray, "cell": p + 1 - 2 * odd}
     across = {"ray": ray + 1 - 2 * yl, "cell": p}
@@ -109,11 +117,14 @@
     r_source = at_cell(2 * odd + 1)
     third = at_cell(6 * odd - 3)
 
-    shifts = set()
+    shifts, split_shifts = set(), set()
     for stage in stages:
         for hop in stage.hops:
             shifts.update((hop, -hop))
-    peers = [sibling, at_cell(2), at_cell(-2), third, across] + [at_z(d) for d in sorted(shifts)]
+        for hop in stage.split_hops:
+            split_shifts.update((hop, -hop))
+    peers = [sibling, at_cell(2), at_cell(-2), third, across] + [at_z(d, yl) for d in sorted(shifts)]
+    peers += [at_z(d, far) for d in sorted(split_shifts)]
     barrier = pltpu.get_barrier_semaphore()
     for peer in peers:
         pl.semaphore_signal(barrier, inc=1, device_id=peer, device_id_type=MESH)
@@ -211,7 +222,7 @@
         return part[0, :, pl.ds(pl.multiple_of(dest * chunk, chunk), chunk), :]
 
     def arrived(stage, k, s):
-        part, sbuf, rbuf, ssem, rsem = stage.refs[:5]
+        rbuf, ssem, rsem = stage.refs[2:5]
         m, slot, width = stage.place[k, s]
         tall = half if stage.near_first else chunk
         rows = stage.items * tall
@@ -223,24 +234,61 @@
 
     def step(stage, s):
         part, sbuf, rbuf, ssem, rsem = stage.refs[:5]
-        for m, hop, members in stage.steps[s]:
+        split_out, split_in, split_send, split_recv = stage.refs[8:]
+        for m, hop, members, split in stage.steps[s]:
             pieces = []
             for k in members:
                 x = own_part(stage, lax.rem(z - stage.paths[k][s] + nz, nz))
                 pieces.append(x if s == 0 else x + arrived(stage, k, s - 1))
-            encode(sbuf, m, pieces)
-            size = 16 + len(members) * pieces[0].shape[0] * pieces[0].shape[1]
-
-            def ends(m=m, size=size):
-                spot = pl.ds(0, size)
-                return sbuf.at[m, spot], rbuf.at[m, spot], ssem.at[m], rsem.at[m]
-
-            send(ends, at_z(hop))
-
-    def summed(stage):
-        x = own_part(stage, z)
+            tall = half if split else pieces[0].shape[1]
+            size = 16 + len(members) * stage.items * tall
+            if not split:
+                encode(sbuf, m, pieces)
+
+                def ends(m=m, size=size):
+                    spot = pl.ds(0, size)
+                    return sbuf.at[m, spot], rbuf.at[m, spot], ssem.at[m], rsem.at[m]
+
+                send(ends, at_z(hop, yl))
+                continue
+            for h in (0, 1):
+                encode(split_out, 2 * m + h, [x[:, h * half : (h + 1) * half] for x in pieces])
+
+                def ends(m=m, size=size, h=h):
+                    spot, to = pl.ds(0, size), 2 * m + yl
+                    return split_out.at[2 * m + h, spot], split_in.at[to, spot], split_send.at[2 * m + h], split_recv.at[to]
+
+                send(ends, at_z(hop, h))
+
+    def lend(stage):
+        part, other, swap = stage.refs[0], stage.refs[5], stage.refs[7]
+
+        def ends():
+            rows = pl.ds(pl.multiple_of(z * chunk + far * half, half), half)
+            return part.at[0, :, rows, :], other, swap.at[0], swap.at[1]
+
+        send(ends, across)
+
+    def finish(stage):
+        part, other, swap = stage.refs[0], stage.refs[5], stage.refs[7]
+        if stage.near_first:
+            x = own_part(stage, z)
+            for k, path in enumerate(stage.paths):
+                x = x + arrived(stage, k, len(path) - 1)
+            return x
+        split_in, split_send, split_recv = stage.refs[9:]
+        await_recv(other, swap.at[0], swap.at[1])
+        x = part[0, :, pl.ds(pl.multiple_of(z * chunk + yl * half, half), half), :] + other[...]
+        rows = stage.items * half
         for k, path in enumerate(stage.paths):
-            x = x + arrived(stage, k, len(path) - 1)
+            m, slot, width = stage.place[k, len(path) - 1]
+            for side in (0, 1):
+                at = 2 * m + side
+                if ("split", at) not in stage.seen:
+                    stage.seen.add(("split", at))
+                    spot = split_in.at[at, pl.ds(0, 16 + width * rows)]
+                    await_recv(spot, split_send.at[at], split_recv.at[at])
+                x = x + decoded(split_in, at, slot, width, rows).reshape(stage.items, half, TILE)
         return x
 
     def cross(stage):
@@ -254,20 +302,6 @@
         rows = stage.items * half * nz
         part[yl] = part[yl] + decoded(near_in, 0, 0, 1, rows).reshape(stage.items, half * nz, TILE)
 
-    def gather(stage):
-        total, other, swap = stage.refs[5:]
-        x = summed(stage)
-        total[0] = x[:, :half]
-        total[1] = x[:, half:]
-        send(lambda: (total.at[far], other, swap.at[0], swap.at[1]), across)
-
-    def finish(stage):
-        if stage.near_first:
-            return summed(stage)
-        total, other, swap = stage.refs[5:]
-        await_recv(other, swap.at[0], swap.at[1])
-        return total[yl] + other[...]
-
     a, b0, b1 = stages[:3]
     visits = stages[3:]
     sib_s = 1 + 2 * odd
@@ -292,9 +326,10 @@
         await_recv(got_z.at[j], in_send.at[j], in_recv.at[j])
         send(lambda: (got_z.at[j], got_sib.at[j], in_send.at[4 + j], in_recv.at[4 + j]), sibling)
 
-    def start_c(j):
-        await_recv(got_sib.at[j], in_send.at[4 + j], in_recv.at[4 + j])
-        multiply(visits[j], own_wt, [got_z.at[j], got_sib.at[j]])
+    def start_c(stage, tiles):
+        for j in tiles:
+            await_recv(got_sib.at[j], in_send.at[4 + j], in_recv.at[4 + j])
+        multiply(stage, own_wt, [got.at[j] for j in tiles for got in (got_z, got_sib)])
 
     def finish_a():
         x = finish(a)
@@ -310,10 +345,11 @@
         for i in range(CT):
             out[b_s, 0, :, i * TILE : (i + 1) * TILE] = b_in[i]
 
-    def finish_c(j):
-        x = finish(visits[j])
-        out[2, 0, :, j * TILE : (j + 1) * TILE] = x[0]
-        out[sib_s, 0, :, j * TILE : (j + 1) * TILE] = x[1]
+    def finish_c(stage, tiles):
+        x = finish(stage)
+        for i, j in enumerate(tiles):
+            out[2, 0, :, j * TILE : (j + 1) * TILE] = x[2 * i]
+            out[sib_s, 0, :, j * TILE : (j + 1) * TILE] = x[2 * i + 1]
 
     events = {}
 
@@ -323,7 +359,7 @@
             found["cross"] = functools.partial(cross, stage)
             found["merge"] = functools.partial(merge, stage)
         else:
-            found["gather"] = functools.partial(gather, stage)
+            found["lend"] = functools.partial(lend, stage)
         for s in range(len(stage.steps)):
             found[f"s{s}"] = functools.partial(step, stage, s)
         for key, event in found.items():
@@ -335,7 +371,9 @@
     events["takeb"] = take_b
     for j in range(CT):
         events[f"pass{j}"] = functools.partial(pass_on, j)
-        add(f"c{j}", visits[j], functools.partial(start_c, j), functools.partial(finish_c, j))
+    for stage, (tiles, _, _, _) in zip(visits, plan[3:]):
+        name = "c" + "".join(map(str, tiles))
+        add(name, stage, functools.partial(start_c, stage, tiles), functools.partial(finish_c, stage, tiles))
     for name in ORDER:
         events.pop(name)()
     assert not events
@@ -372,19 +410,26 @@
         dma((9,)),
     ]
     half = chunk // 2
-    for name, items, stride, mirror, near_first in plan:
+    for tiles, stride, mirror, near_first in plan:
+        items = items_of(tiles)
         stage = Stage(items, nz, stride, mirror, near_first, None)
-        rows = 16 + stage.widest * items * (half if near_first else chunk)
+        count, splits = stage.count[0], max(stage.count[1], 1)
+        rows = 16 + stage.widest[0] * items * (half if near_first else chunk)
         near = (1, 16 + items * half * nz, TILE)
+        split = (2 * splits, 16 + stage.widest[1] * items * half, TILE)
         scratch += [
             pltpu.VMEM((2, items, half * nz, TILE) if near_first else (1, items, chunk * nz, TILE), f32),
-            pltpu.VMEM((stage.count, rows, TILE), jnp.int16),
-            pltpu.VMEM((stage.count, rows, TILE), jnp.int16),
-            dma((stage.count,)),
-            dma((stage.count,)),
-            pltpu.VMEM(near, jnp.int16) if near_first else pltpu.VMEM((2, items, half, TILE), f32),
+            pltpu.VMEM((count, rows, TILE), jnp.int16),
+            pltpu.VMEM((count, rows, TILE), jnp.int16),
+            dma((count,)),
+            dma((count,)),
             pltpu.VMEM(near, jnp.int16) if near_first else pltpu.VMEM((items, half, TILE), f32),
+            pltpu.VMEM(near, jnp.int16),
             dma((2,)),
+            pltpu.VMEM(split, jnp.int16),
+            pltpu.VMEM(split, jnp.int16),
+            dma((2 * splits,)),
+            dma((2 * splits,)),
         ]
     scratch += [
         pltpu.VMEM((CT, chunk // 2, TILE), f32),

time: 67 us -> 67.2 us (level)
  the two profiles are of different devices: /device:TPU:32 before, /device:TPU:8 now
where the time goes in v5:
time: 67.2 us; the launch traced here: 67 us
  Pallas kernels  65.6 us (98%)
  local copies, waits for them, and re-layouts  1.35 us (2%)
    pallas_call x1, Pallas kernels, body(): pl.pallas_call(functools.partial(kernel, nz, plan), out_shape=jax.ShapeDt...  65.6 us
    unnamed x7, local copies, waits for them, and re-layouts  1.35 us

profile of v5, /device:TPU:8, one launch (start us, length us, event | category | flops | bytes accessed | tf_op | source)
XLA Modules:
  0.0 67.0 jit_solution(5776002324205121418)
XLA Ops:
  0.0 0.0 copy-start
  0.0 0.0 copy-start.1
  0.0 0.0 copy-start.2
  0.0 0.7 %copy-done = f32[1024]{0:T(1024)S(1)} copy-done((f32[1024]{0:T(1024)S(1)}, f32[1024]{0:T(1024)}, u32[]{:S(2)}) %copy-start) | copy-done | bytes 4120
  0.7 0.0 copy-done.1
  0.7 0.0 copy-done.2
  0.7 65.6 %shard_map.46 = f32[4,1,16,512]{3,2,1,0:T(8,128)S(1)} custom-call(bf16[8,4,128,128]{3,2,1,0:T(8,128)(2,1)} %bitcast.9, s32[4,8]{1,0:T(4,128)S(1)} %bitcast.7, s32[8]{0:T(128)S(1)} %bitcast.8, f32[8,128]{1,0:T(8,128)S(1)} %bitcast.6), custom_call_target="tpu_custom_call" | custom-call | tf_op jit(solution)/shard_map/pallas_call | solution.py:441
  66.3 0.7 copy.6
Async XLA Ops:
  0.0 0.7 %copy-start = (f32[1024]{0:T(1024)S(1)}, f32[1024]{0:T(1024)}, u32[]{:S(2)}) copy-start(f32[1024]{0:T(1024)} %param.7) | copy-start | bytes 12292
  0.0 0.7 %copy-start.1 = (s32[8,1,4]{0,2,1:T(4,128)S(1)}, s32[8,1,4]{0,2,1:T(4,128)}, u32[]{:S(2)}) copy-start(s32[8,1,4]{0,2,1:T(4,128)} %param.5) | copy-start | bytes 388
  0.0 0.7 %copy-start.2 = (s32[8,1]{0,1:T(1,128)S(1)}, s32[8,1]{0,1:T(1,128)}, u32[]{:S(2)}) copy-start(s32[8,1]{0,1:T(1,128)} %param.6) | copy-start | bytes 100
